TPU v7x, 512 devices: a whole 4x8x8 slice. The times are simulated.
512 devices in a mesh: grp: 32 (over y, x), mlp: 16 (over z, core).
Axes of the slice: x: 4, y: 8, z: 8, core: 2. Of those that a mesh axis runs over, the one named last changes fastest.
Arguments:
- queries: bfloat16 [32, 128, 4096], P('grp'), may hold values from -70 to 70
- fresh_kv: bfloat16 [32, 128, 1024], P('grp', 'mlp'), may hold values from -5 to 5
- kv_pages: bfloat16 [32, 32, 128, 1024], P('grp', 'mlp'), may hold values from -5 to 5
- residual: bfloat16 [32, 128, 4096], P('grp'), may hold values from -3 to 3
- norm_gain: float32 [4096], replicated, may hold values from 0.5 to 1.5
- out_weight: bfloat16 [4096, 4096], P('mlp', 'grp'), may hold values from -0.09375 to 0.09375
- gate_weight: bfloat16 [4096, 6144], P('grp', 'mlp'), may hold values from -0.09375 to 0.09375
- up_weight: bfloat16 [4096, 6144], P('grp', 'mlp'), may hold values from -0.09375 to 0.09375
- down_weight: bfloat16 [6144, 4096], P('mlp', 'grp'), may hold values from -0.078125 to 0.078125
- page_table: int32 [32, 16, 12], P('grp'), may hold values from -1 to 31, as said below
- shared_pages: int32 [32, 4], P('grp'), may hold values from 0 to 31, as said below
- cache_lens: int32 [32, 16], P('grp'), may hold values from 513 to 2048, as said below
- prefill_offsets: int32 [32], P('grp'), may hold values from 1 to 512
Outputs:
- layer_out: bfloat16 [32, 128, 4096], P('grp', 'mlp')
Inputs may be any that keep to these rules, and one draw needn't show every extreme that they name: `page_table`: row d lists the pool pages that hold decode d's tokens after the shared prompt, in order, and -1 after its last page; no page appears twice in a group, and none is also a shared page. `shared_pages`: the pool pages of the group's shared prompt in order; they are the first 4 pages of every request of the group. `cache_lens`: decode d's cached tokens fill exactly its listed pages after the 4 shared pages; in every group one decode has the most.
All inputs are finite; a program needn't handle non-finite values.
Results may differ from a plain program's by a relative error of at most 0.029.
Values may be sent and summed in bfloat16 or wider, within the bound.
No kernel may reach another device: no remote copies, remote signals or barrier semaphores. Data moves between devices by JAX's collectives and lax.ppermute only.
A program may use at most 128 MiB of HBM per device.

v0:
```python
import jax
import jax.numpy as jnp
from jax import lax
from jax.sharding import PartitionSpec as P

HEADS = 32
KV_HEADS = 4
HEAD = 128
PAGE = 128
SHARED_PAGES = 4
PRIVATE_PAGES = 12
DECODES = 16
PREFILL = 112
ROWS = 128
NEG_FILL = -1e30
EPSILON = 1e-05


def merged(shard, axis, combine):
    everything = jax.tree.map(lambda part: lax.all_gather(part, axis), shard)
    leading = jax.tree.map(lambda part: part[0], everything)

    def step(k, so_far):
        return combine(so_far, jax.tree.map(lambda part: part[k], everything))

    return lax.fori_loop(1, lax.axis_size(axis), step, leading)


def page_layout(page_ids, table_group, shared_group):
    shared_match = shared_group[None, :] == page_ids[:, None]
    is_shared = jnp.any(shared_match, axis=1)
    shared_slot = jnp.sum(
        jnp.where(shared_match, jnp.arange(SHARED_PAGES, dtype=jnp.int32)[None, :], 0),
        axis=1,
        dtype=jnp.int32,
    )
    own_match = table_group[None, :, :] == page_ids[:, None, None]
    owner_id = (
        jnp.sum(
            jnp.where(own_match, jnp.arange(DECODES, dtype=jnp.int32)[None, :, None] + 1, 0),
            axis=(1, 2),
            dtype=jnp.int32,
        )
        - 1
    )
    own_slot = jnp.sum(
        jnp.where(own_match, jnp.arange(PRIVATE_PAGES, dtype=jnp.int32)[None, None, :], 0),
        axis=(1, 2),
        dtype=jnp.int32,
    )
    page_base = jnp.where(is_shared, shared_slot * PAGE, (SHARED_PAGES + own_slot) * PAGE)
    key_pos = (page_base[:, None] + jnp.arange(PAGE, dtype=jnp.int32)[None, :]).reshape(-1)
    key_shared = jnp.repeat(is_shared, PAGE)
    key_owner = jnp.repeat(jnp.where(is_shared, -1, owner_id), PAGE)
    return (key_pos, key_shared, key_owner)


def row_layout(lens_group, offset_value):
    row_ids = jnp.arange(ROWS, dtype=jnp.int32)
    is_prefill = row_ids < PREFILL
    decode_id = jnp.where(is_prefill, -2, row_ids - PREFILL)
    picked = decode_id[:, None] == jnp.arange(DECODES, dtype=jnp.int32)[None, :]
    decode_limit = jnp.sum(jnp.where(picked, lens_group[None, :], 0), axis=1, dtype=jnp.int32)
    limit = jnp.where(is_prefill, offset_value, decode_limit)
    return (row_ids, is_prefill, decode_id, limit)


def cache_visible(key_pos, key_shared, key_owner, decode_id, limit):
    belongs = key_shared[None, :] | (key_owner[None, :] == decode_id[:, None])
    return belongs & (key_pos[None, :] < limit[:, None])


def fresh_visible(key_rows, row_ids, is_prefill):
    before = (key_rows[None, :] < PREFILL) & (key_rows[None, :] <= row_ids[:, None])
    return jnp.where(is_prefill[:, None], before, key_rows[None, :] == row_ids[:, None])


def rms_norm(values, norm_gain):
    return (
        values * lax.rsqrt(jnp.mean(values * values, axis=1, keepdims=True) + EPSILON) * norm_gain
    ).astype(jnp.bfloat16)


def combine_parts(earlier_part, later_part):
    peak_one, total_one, mixed_one = earlier_part
    peak_two, total_two, mixed_two = later_part
    row_peak = jnp.maximum(peak_one, peak_two)
    factor_one = jnp.exp(peak_one - row_peak)
    factor_two = jnp.exp(peak_two - row_peak)
    row_total = total_one * factor_one + total_two * factor_two
    row_number, head_number = row_peak.shape
    weighted = (
        mixed_one.reshape(row_number, head_number, -1) * factor_one[:, :, None]
        + mixed_two.reshape(row_number, head_number, -1) * factor_two[:, :, None]
    )
    return (row_peak, row_total, weighted.reshape(row_number, -1))


def local(
    queries,
    fresh_kv,
    kv_pages,
    residual,
    norm_gain,
    out_weight,
    gate_weight,
    up_weight,
    down_weight,
    page_table,
    shared_pages,
    cache_lens,
    prefill_offsets,
):
    out_rows, gate_cols, up_cols, down_rows = (
        lax.all_gather(out_weight, "grp", axis=1, tiled=True),
        lax.all_gather(gate_weight, "grp", axis=0, tiled=True),
        lax.all_gather(up_weight, "grp", axis=0, tiled=True),
        lax.all_gather(down_weight, "grp", axis=1, tiled=True),
    )
    mlp_index = lax.axis_index("mlp")
    pool_pages = kv_pages.shape[1]
    own_count = fresh_kv.shape[1]
    page_ids = mlp_index * pool_pages + jnp.arange(pool_pages, dtype=jnp.int32)
    key_rows = mlp_index * own_count + jnp.arange(own_count, dtype=jnp.int32)
    key_pos, key_shared, key_owner = page_layout(page_ids, page_table[0], shared_pages[0])
    row_ids, is_prefill, decode_id, limit = row_layout(cache_lens[0], prefill_offsets[0])
    cache_seen = cache_visible(key_pos, key_shared, key_owner, decode_id, limit)
    fresh_seen = fresh_visible(key_rows, row_ids, is_prefill)
    cached = kv_pages[0].reshape(pool_pages * PAGE, 2, KV_HEADS, HEAD)
    fresh = fresh_kv[0].reshape(own_count, 2, KV_HEADS, HEAD)
    grouped = HEADS // KV_HEADS
    query_heads = queries[0].reshape(ROWS, KV_HEADS, grouped, HEAD)
    score_scale = HEAD ** (-0.5)
    peak_list = []
    total_list = []
    mixed_list = []
    for head_index in range(KV_HEADS):
        query_block = query_heads[:, head_index]
        cache_scores = (
            jnp.einsum(
                "rgh,kh->rgk",
                query_block,
                cached[:, 0, head_index],
                preferred_element_type=jnp.float32,
            )
            * score_scale
        )
        fresh_scores = (
            jnp.einsum(
                "rgh,kh->rgk",
                query_block,
                fresh[:, 0, head_index],
                preferred_element_type=jnp.float32,
            )
            * score_scale
        )
        cache_scores = jnp.where(cache_seen[:, None, :], cache_scores, NEG_FILL)
        fresh_scores = jnp.where(fresh_seen[:, None, :], fresh_scores, NEG_FILL)
        row_peak = jnp.maximum(jnp.max(cache_scores, axis=2), jnp.max(fresh_scores, axis=2))
        cache_exps = jnp.where(
            cache_seen[:, None, :], jnp.exp(cache_scores - row_peak[:, :, None]), 0.0
        )
        fresh_exps = jnp.where(
            fresh_seen[:, None, :], jnp.exp(fresh_scores - row_peak[:, :, None]), 0.0
        )
        row_total = jnp.sum(cache_exps, axis=2) + jnp.sum(fresh_exps, axis=2)
        weighted = jnp.einsum(
            "rgk,kh->rgh",
            cache_exps.astype(jnp.bfloat16),
            cached[:, 1, head_index],
            preferred_element_type=jnp.float32,
        )
        weighted = weighted + jnp.einsum(
            "rgk,kh->rgh",
            fresh_exps.astype(jnp.bfloat16),
            fresh[:, 1, head_index],
            preferred_element_type=jnp.float32,
        )
        peak_list.append(row_peak)
        total_list.append(row_total)
        mixed_list.append(weighted)
    row_peak = jnp.stack(peak_list, axis=1).reshape(ROWS, HEADS)
    row_total = jnp.stack(total_list, axis=1).reshape(ROWS, HEADS)
    weighted = jnp.stack(mixed_list, axis=1).reshape(ROWS, HEADS * HEAD)
    row_peak, row_total, weighted = merged((row_peak, row_total, weighted), "mlp", combine_parts)
    attended = (
        (weighted.reshape(ROWS, HEADS, HEAD) / row_total[:, :, None])
        .reshape(ROWS, HEADS * HEAD)
        .astype(jnp.bfloat16)
    )
    feature_count = out_rows.shape[0]
    own_features = lax.dynamic_slice_in_dim(attended, mlp_index * feature_count, feature_count, 1)
    row_begin = mlp_index * own_count
    projected = lax.psum(
        jnp.dot(own_features, out_rows, preferred_element_type=jnp.float32).astype(jnp.bfloat16),
        "mlp",
    ).astype(jnp.float32)
    updated = residual[0].astype(jnp.float32) + projected
    normed = rms_norm(updated, norm_gain)
    carried_rows = lax.dynamic_slice_in_dim(updated, row_begin, own_count, 0)
    gate_act = jnp.dot(normed, gate_cols, preferred_element_type=jnp.float32)
    up_act = jnp.dot(normed, up_cols, preferred_element_type=jnp.float32)
    hidden = (jax.nn.silu(gate_act) * up_act).astype(jnp.bfloat16)
    returned = lax.psum_scatter(
        jnp.dot(hidden, down_rows, preferred_element_type=jnp.float32).astype(jnp.bfloat16),
        "mlp",
        scatter_dimension=0,
        tiled=True,
    ).astype(jnp.float32)
    return (carried_rows + returned).astype(jnp.bfloat16)[None]


def solution(mesh):
    placed = (
        P("grp", None, None),
        P("grp", "mlp", None),
        P("grp", "mlp", None, None),
        P("grp", None, None),
        P(),
        P("mlp", "grp"),
        P("grp", "mlp"),
        P("grp", "mlp"),
        P("mlp", "grp"),
        P("grp", None, None),
        P("grp", None),
        P("grp", None),
        P("grp"),
    )
    return jax.shard_map(
        local, mesh=mesh, in_specs=placed, out_specs=P("grp", "mlp", None), check_vma=False
    )
```

profile of v0, /device:TPU:2, one launch (start us, length us, event | category | flops | bytes accessed | tf_op | source)
XLA Modules:
  0.0 786.7 jit_solution(5587190281900795073)
XLA Ops:
  6.6 0.9 compare_reduce_fusion
  7.5 0.8 fusion.85
  8.3 1.6 copy.59
  10.1 0.8 fusion.107
  14.3 1.6 fusion.99
  16.5 1.0 fusion.106
  17.5 1.9 fusion.104
  19.4 1.8 copy.89
  21.2 2.0 fusion.102
  23.2 0.9 copy.90
  24.1 2.9 fusion.100
  28.3 1.0 fusion.10
  29.7 1.0 fusion.9
  31.2 0.9 fusion.8
  32.6 0.9 fusion.7
  33.8 1.8 copy.72
  37.2 2.4 fusion.17
  39.7 24.5 %all_gather.22 = f32[16,128,32]{1,2,0:T(8,128)S(1)} all-gather(f32[1,128,32]{1,2,0:T(8,128)S(1)} %maximum_bitcast_fusion.1), channel_id=1, replica_groups=mesh['grp'=32,'mlp'=16] {'mlp'}, dimensions={0}, use_global_device_ids=true | all-gather | bytes 278528 | tf_op jit(solution)/shard_map/all_gather | solution.py:20
  64.3 16.6 %all_gather.21 = f32[16,128,32]{1,2,0:T(8,128)S(1)} all-gather(f32[1,128,32]{1,2,0:T(8,128)S(1)} %maximum_bitcast_fusion), channel_id=1, replica_groups=mesh['grp'=32,'mlp'=16] {'mlp'}, dimensions={0}, use_global_device_ids=true | all-gather | bytes 278528 | tf_op jit(solution)/shard_map/all_gather | solution.py:20
  81.0 139.0 %all-gather.6.cloned.1.call-done = f32[16,128,4096]{2,1,0:T(8,128)} async-done(((f32[1,128,4096]{2,1,0:T(8,128)}), f32[16,128,4096]{2,1,0:T(8,128)}) %all-gather.6.cloned.1.call-update) | async-done | bytes 33554448 | tf_op jit(solution)/shard_map/all_gather | solution.py:20
  220.0 1.7 slice_bitcast_fusion
  221.8 108.8 %while.19 = (s32[]{:T(128)}, f32[128,32]{1,0:T(8,128)S(1)}, f32[128,32]{1,0:T(8,128)S(1)}, f32[128,4096]{1,0:T(8,128)S(1)}, f32[16,128,32]{1,2,0:T(8,128)S(1)}, ...) while((s32[]{:T(128)}, f32[128,32]{1,0:T(8,128)S(1)}, ...), condition=%wide.region_22.23_spmd, body=%wide.region_21.22_spmd.sunk | while | flops 1597445 | bytes 14975127 | solution.py:26
  223.3 5.7 fusion.115
  230.6 5.7 fusion.115
  237.8 5.7 fusion.115
  245.1 5.7 fusion.115
  252.3 5.7 fusion.115
  259.6 5.7 fusion.115
  266.8 5.7 fusion.115
  274.1 5.7 fusion.115
  281.3 5.7 fusion.115
  288.6 5.7 fusion.115
  295.9 5.7 fusion.115
  303.1 5.7 fusion.115
  310.4 5.7 fusion.115
  317.6 5.7 fusion.115
  324.9 5.7 fusion.115
  331.2 3.0 copy.115
  334.2 3.2 convolution_convert_fusion.1
  339.2 114.0 %all-reduce.2.cloned.1.call-done = bf16[128,4096]{1,0:T(8,128)(2,1)} async-done(((bf16[128,4096]{1,0:T(8,128)(2,1)}), bf16[128,4096]{1,0:T(8,128)(2,1)}) %all-reduce.2.cloned.1.call-update) | async-done | bytes 1048592 | tf_op jit(solution)/shard_map/psum | solution.py:194
  453.3 3.0 convert_add_fusion
  456.2 84.0 %all-gather.10.cloned.1.call-done = bf16[4096,384]{1,0:T(8,128)(2,1)} async-done(((bf16[128,384]{1,0:T(8,128)(2,1)}), bf16[4096,384]{1,0:T(8,128)(2,1)}) %all-gather.10.cloned.1.call-update) | async-done | bytes 3145744 | tf_op jit(solution)/shard_map/all_gather | solution.py:116
  540.3 2.6 fusion.97
  542.9 83.0 %all-gather.12.cloned.1.call-done = bf16[4096,384]{1,0:T(8,128)(2,1)} async-done(((bf16[128,384]{1,0:T(8,128)(2,1)}), bf16[4096,384]{1,0:T(8,128)(2,1)}) %all-gather.12.cloned.1.call-update) | async-done | bytes 3145744 | tf_op jit(solution)/shard_map/all_gather | solution.py:117
  625.9 86.5 %all-gather.14.cloned.1.call-done = bf16[384,4096]{1,0:T(8,128)(2,1)} async-done(((bf16[384,128]{1,0:T(8,128)(2,1)}), bf16[384,4096]{1,0:T(8,128)(2,1)}) %all-gather.14.cloned.1.call-update) | async-done | bytes 3145744 | tf_op jit(solution)/shard_map/all_gather | solution.py:118
  712.5 5.3 convolution_convert_fusion
  717.8 60.5 %reduce-scatter.2.cloned.1.call-done = bf16[8,4096]{1,0:T(8,128)(2,1)} async-done(((bf16[128,4096]{1,0:T(8,128)(2,1)}), bf16[8,4096]{1,0:T(8,128)(2,1)}) %reduce-scatter.2.cloned.1.call-update) | async-done | bytes 65552 | tf_op jit(solution)/shard_map/reduce_scatter | solution.py:204
  778.2 1.6 fusion.51
  (190 shorter events, 32.3 us)
Async XLA Ops:
  6.5 3.5 copy-start.16
  6.5 6.6 copy-start.15
  6.5 7.4 copy-start.8
  6.5 213.5 %all-gather.6.cloned.1.call-start = ((), (), s32[]{:S(2)}) async-start(), calls=%async_computation.1 | async-start | bytes 35651584 | tf_op jit(solution)/shard_map/all_gather | solution.py:20
  10.0 7.5 copy-start.7
  11.7 4.6 copy-start.20
  19.4 9.8 %copy-start.2 = (f32[128,8,256]{2,0,1:T(8,128)}, f32[128,8,256]{2,0,1:T(8,128)S(1)}, u32[]{:S(2)}) copy-start(f32[128,8,256]{2,0,1:T(8,128)S(1)} %get-tuple-element.256) | copy-start | bytes 3145732
  23.2 7.6 copy-start.4
  24.1 5.2 copy-start.10
  27.1 2.1 copy-start.19
  27.8 1.9 copy-start.11
  28.2 2.5 copy-start.18
  28.2 2.6 copy-start.9
  29.3 1.9 copy-start.12
  29.7 2.5 copy-start.17
  29.7 2.5 copy-start.6
  30.8 1.8 copy-start.13
  35.6 1.2 copy-start.3
  35.6 1.5 copy-start.5
  35.7 298.6 %all-gather.8.cloned.1.call-start = ((), (), s32[]{:S(2)}) async-start(), calls=%async_computation.2 | async-start | bytes 2162688 | tf_op jit(solution)/shard_map/all_gather | solution.py:115
  36.4 416.8 %all-reduce.2.cloned.1.call-start = ((), (), s32[]{:S(2)}) async-start(), calls=%async_computation.3 | async-start | bytes 2097152 | tf_op jit(solution)/shard_map/psum | solution.py:194
  334.2 119.0 %copy-start = (bf16[1,128,4096]{2,1,0:T(8,128)(2,1)S(1)}, bf16[1,128,4096]{2,1,0:T(8,128)(2,1)}, u32[]{:S(2)}) copy-start(bf16[1,128,4096]{2,1,0:T(8,128)(2,1)} %param.18) | copy-start | bytes 3145732
  337.4 202.8 %all-gather.10.cloned.1.call-start = ((), (), s32[]{:S(2)}) async-start(), calls=%async_computation.4 | async-start | bytes 3244032 | tf_op jit(solution)/shard_map/all_gather | solution.py:116
  338.0 287.9 %all-gather.12.cloned.1.call-start = ((), (), s32[]{:S(2)}) async-start(), calls=%async_computation.5 | async-start | bytes 3244032 | tf_op jit(solution)/shard_map/all_gather | solution.py:117
  338.6 373.9 %all-gather.14.cloned.1.call-start = ((), (), s32[]{:S(2)}) async-start(), calls=%async_computation.6 | async-start | bytes 3244032 | tf_op jit(solution)/shard_map/all_gather | solution.py:118
  339.2 201.1 %copy-start.14 = (f32[4096]{0:T(1024)S(1)}, f32[4096]{0:T(1024)}, u32[]{:S(2)}) copy-start(f32[4096]{0:T(1024)} %param.19) | copy-start | bytes 49156
  339.2 439.1 %reduce-scatter.2.cloned.1.call-start = ((), (), s32[]{:S(2)}) async-start(), calls=%async_computation.7 | async-start | bytes 1114112 | tf_op jit(solution)/shard_map/reduce_scatter | solution.py:204
  453.2 87.0 %copy-start.1 = (bf16[128,4096]{1,0:T(8,128)(2,1)S(1)}, bf16[128,4096]{1,0:T(8,128)(2,1)}, u32[]{:S(2)}) copy-start(bf16[128,4096]{1,0:T(8,128)(2,1)} %all-reduce.2.cloned.1.call-done) | copy-start | bytes 3145732
Sparse Core Ops, SparseCore 0:
  35.8 184.2 all-gather.5
  223.1 77.9 all-gather.7
  337.5 115.6 all-reduce.1
  456.7 83.4 all-gather.9
  543.8 82.1 all-gather.11
  629.3 83.1 all-gather.13
  717.9 60.2 reduce-scatter.1
where the time goes:
time: 788 us; the launch traced here: 787 us
  waiting for transfers between devices  569 us (72%)
  other arithmetic  97.4 us (12%)
  blocking collectives  41.1 us (5%)
  local copies, waits for them, and re-layouts  35.7 us (5%)
  matrix products  27.6 us (4%)
  between operations  14.6 us (2%)
    all_gather x1, waiting for transfers between devices, merged(): everything = jax.tree.map(lambda part: lax.all_gather(part, axis), shard)  139 us
    psum x1, waiting for transfers between devices, local(): lax.psum(jnp.dot(own_features, out_rows, preferred_element_type=jnp.float...  114 us
    all_gather x1, waiting for transfers between devices, local(): lax.all_gather(down_weight, 'grp', axis=1, tiled=True)  86.5 us
    add x15, other arithmetic, combine_parts(): mixed_one.reshape(row_number, head_number, -1) * factor_one[:, :, None]  86.1 us
    all_gather x1, waiting for transfers between devices, local(): lax.all_gather(gate_weight, 'grp', axis=0, tiled=True)  84 us
    all_gather x1, waiting for transfers between devices, local(): lax.all_gather(up_weight, 'grp', axis=0, tiled=True)  83 us
    reduce_scatter x1, waiting for transfers between devices, local(): lax.psum_scatter(jnp.dot(hidden, down_rows, preferred_element_type=jnp.fl...  60.5 us
    all_gather x2, blocking collectives, merged(): everything = jax.tree.map(lambda part: lax.all_gather(part, axis), shard)  41.1 us
  transfers between devices with their start and end apart: 7, of which 6 were waited for; matrix products, arithmetic and copies ran while one was open for 15% of the time, Pallas kernels for 0%

commit v1 on v0

--- a/solution.py
+++ b/solution.py
@@ -114,7 +114,9 @@
     out_rows, gate_cols, up_cols, down_rows = (
         lax.all_gather(out_weight, "grp", axis=1, tiled=True),
         lax.all_gather(gate_weight, "grp", axis=0, tiled=True),
-        lax.all_gather(up_weight, "grp", axis=0, tiled=True),
+        jnp.concatenate(
+            lax.all_to_all(jnp.stack([up_weight] * lax.axis_size("grp")), "grp", 0, 0), axis=0
+        ),
         lax.all_gather(down_weight, "grp", axis=1, tiled=True),
     )
     mlp_index = lax.axis_index("mlp")

time: 788 us -> 703 us (0.89)
  the two profiles are of different devices: /device:TPU:2 before, /device:TPU:16 now
where the time goes in v1:
time: 703 us; the launch traced here: 702 us
  waiting for transfers between devices  472 us (67%)
  other arithmetic  97.6 us (14%)
  blocking collectives  41.1 us (6%)
  local copies, waits for them, and re-layouts  37.9 us (5%)
  matrix products  27.9 us (4%)
  between operations  14.6 us (2%)
  starting transfers between devices  10 us (1%)
    all_gather x1, waiting for transfers between devices, merged(): everything = jax.tree.map(lambda part: lax.all_gather(part, axis), shard)  139 us
    psum x1, waiting for transfers between devices, local(): lax.psum(jnp.dot(own_features, out_rows, preferred_element_type=jnp.float...  104 us
    add x15, other arithmetic, combine_parts(): mixed_one.reshape(row_number, head_number, -1) * factor_one[:, :, None]  86.1 us
    all_gather x1, waiting for transfers between devices, local(): lax.all_gather(gate_weight, 'grp', axis=0, tiled=True)  84.2 us
    all_gather x1, waiting for transfers between devices, local(): lax.all_gather(down_weight, 'grp', axis=1, tiled=True)  81.3 us
    reduce_scatter x1, waiting for transfers between devices, local(): lax.psum_scatter(jnp.dot(hidden, down_rows, preferred_element_type=jnp.fl...  62 us
    all_gather x2, blocking collectives, merged(): everything = jax.tree.map(lambda part: lax.all_gather(part, axis), shard)  41.1 us
  transfers between devices with their start and end apart: 7, of which 5 were waited for; matrix products, arithmetic and copies ran while one was open for 18% of the time, Pallas kernels for 0%

profile of v1, /device:TPU:16, one launch (start us, length us, event | category | flops | bytes accessed | tf_op | source)
XLA Modules:
  0.0 702.1 jit_solution(1852616128215169947)
XLA Ops:
  6.6 0.9 compare_reduce_fusion
  8.3 1.6 copy.59
  10.1 0.8 fusion.107
  14.3 1.6 fusion.99
  16.5 1.0 fusion.106
  17.5 1.9 fusion.104
  19.4 1.8 copy.89
  21.2 2.0 fusion.102
  23.2 0.9 copy.90
  24.1 2.9 fusion.100
  28.3 1.0 fusion.10
  29.7 1.0 fusion.9
  31.2 0.9 fusion.8
  32.6 0.9 fusion.7
  33.8 1.8 copy.72
  37.2 2.4 fusion.17
  39.7 24.5 %all_gather.19 = f32[16,128,32]{1,2,0:T(8,128)S(1)} all-gather(f32[1,128,32]{1,2,0:T(8,128)S(1)} %maximum_bitcast_fusion.1), channel_id=1, replica_groups=mesh['grp'=32,'mlp'=16] {'mlp'}, dimensions={0}, use_global_device_ids=true | all-gather | bytes 278528 | tf_op jit(solution)/shard_map/all_gather | solution.py:20
  64.3 16.6 %all_gather.18 = f32[16,128,32]{1,2,0:T(8,128)S(1)} all-gather(f32[1,128,32]{1,2,0:T(8,128)S(1)} %maximum_bitcast_fusion), channel_id=1, replica_groups=mesh['grp'=32,'mlp'=16] {'mlp'}, dimensions={0}, use_global_device_ids=true | all-gather | bytes 278528 | tf_op jit(solution)/shard_map/all_gather | solution.py:20
  81.0 138.9 %all-gather.5.cloned.1.call-done = f32[16,128,4096]{2,1,0:T(8,128)} async-done(((f32[1,128,4096]{2,1,0:T(8,128)}), f32[16,128,4096]{2,1,0:T(8,128)}) %all-gather.5.cloned.1.call-update) | async-done | bytes 33554448 | tf_op jit(solution)/shard_map/all_gather | solution.py:20
  219.9 1.7 slice_bitcast_fusion
  221.6 108.8 %while.19 = (s32[]{:T(128)}, f32[128,32]{1,0:T(8,128)S(1)}, f32[128,32]{1,0:T(8,128)S(1)}, f32[128,4096]{1,0:T(8,128)S(1)}, f32[16,128,32]{1,2,0:T(8,128)S(1)}, ...) while((s32[]{:T(128)}, f32[128,32]{1,0:T(8,128)S(1)}, ...), condition=%wide.region_22.23_spmd, body=%wide.region_21.22_spmd.sunk | while | flops 1597445 | bytes 14975127 | solution.py:26
  223.1 5.7 fusion.115
  230.4 5.7 fusion.115
  237.7 5.7 fusion.115
  244.9 5.7 fusion.115
  252.2 5.7 fusion.115
  259.4 5.7 fusion.115
  266.7 5.7 fusion.115
  273.9 5.7 fusion.115
  281.2 5.7 fusion.115
  288.4 5.7 fusion.115
  295.7 5.7 fusion.115
  303.0 5.7 fusion.115
  310.2 5.7 fusion.115
  317.5 5.7 fusion.115
  324.7 5.7 fusion.115
  331.1 3.0 copy.115
  334.1 3.1 convolution_convert_fusion.1
  337.8 2.2 stack.23
  340.0 9.8 %all-to-all-start = ((bf16[32,128,384]{2,1,0:T(8,128)(2,1)}), bf16[32,128,384]{2,1,0:T(8,128)(2,1)S(1)}, u32[]{:S(2)}, u32[]{:S(2)}) async-start(bf16[32,128,384]{2,1,0:T(8,128)(2,1)} %stack.23), calls=%async_computation | async-start | bytes 6291456 | tf_op jit(solution)/shard_map/all_to_all | solution.py:118
  350.5 104.2 %all-reduce.2.cloned.1.call-done = bf16[128,4096]{1,0:T(8,128)(2,1)} async-done(((bf16[128,4096]{1,0:T(8,128)(2,1)}), bf16[128,4096]{1,0:T(8,128)(2,1)}) %all-reduce.2.cloned.1.call-update) | async-done | bytes 1048592 | tf_op jit(solution)/shard_map/psum | solution.py:196
  454.6 3.2 convert_add_fusion
  457.8 84.2 %all-gather.9.cloned.1.call-done = bf16[4096,384]{1,0:T(8,128)(2,1)} async-done(((bf16[128,384]{1,0:T(8,128)(2,1)}), bf16[4096,384]{1,0:T(8,128)(2,1)}) %all-gather.9.cloned.1.call-update) | async-done | bytes 3145744 | tf_op jit(solution)/shard_map/all_gather | solution.py:116
  542.0 3.3 fusion.97
  545.3 81.3 %all-gather.11.cloned.1.call-done = bf16[384,4096]{1,0:T(8,128)(2,1)} async-done(((bf16[384,128]{1,0:T(8,128)(2,1)}), bf16[384,4096]{1,0:T(8,128)(2,1)}) %all-gather.11.cloned.1.call-update) | async-done | bytes 3145744 | tf_op jit(solution)/shard_map/all_gather | solution.py:120
  626.7 5.0 convolution_convert_fusion
  631.7 62.0 %reduce-scatter.2.cloned.1.call-done = bf16[8,4096]{1,0:T(8,128)(2,1)} async-done(((bf16[128,4096]{1,0:T(8,128)(2,1)}), bf16[8,4096]{1,0:T(8,128)(2,1)}) %reduce-scatter.2.cloned.1.call-update) | async-done | bytes 65552 | tf_op jit(solution)/shard_map/reduce_scatter | solution.py:206
  693.6 1.6 fusion.51
  (188 shorter events, 32.6 us)
Async XLA Ops:
  6.5 3.5 copy-start.15
  6.5 6.6 copy-start.14
  6.5 7.4 %copy-start.6 = (bf16[1,2,128,1024]{3,2,1,0:T(8,128)(2,1)S(1)}, bf16[1,2,128,1024]{3,2,1,0:T(8,128)(2,1)}, u32[]{:S(2)}) copy-start(bf16[1,2,128,1024]{3,2,1,0:T(8,128)(2,1)} %param.17) | copy-start | bytes 1572868
  6.5 213.3 %all-gather.5.cloned.1.call-start = ((), (), s32[]{:S(2)}) async-start(), calls=%async_computation.2 | async-start | bytes 35651584 | tf_op jit(solution)/shard_map/all_gather | solution.py:20
  10.0 7.5 %copy-start.5 = (bf16[1,128,4096]{1,2,0:T(8,128)(2,1)}, bf16[1,128,4096]{1,2,0:T(8,128)(2,1)S(1)}, u32[]{:S(2)}) copy-start(bf16[1,128,4096]{1,2,0:T(8,128)(2,1)S(1)} %copy.59) | copy-start | bytes 3145732
  11.7 4.6 copy-start.19
  19.4 9.8 %copy-start = (f32[128,8,256]{2,0,1:T(8,128)}, f32[128,8,256]{2,0,1:T(8,128)S(1)}, u32[]{:S(2)}) copy-start(f32[128,8,256]{2,0,1:T(8,128)S(1)} %get-tuple-element.256) | copy-start | bytes 3145732
  23.2 7.6 %copy-start.2 = (f32[128,8,256]{2,0,1:T(8,128)}, f32[128,8,256]{2,0,1:T(8,128)S(1)}, u32[]{:S(2)}) copy-start(f32[128,8,256]{2,0,1:T(8,128)S(1)} %get-tuple-element.252) | copy-start | bytes 3145732
  24.1 5.2 copy-start.8
  27.1 2.1 copy-start.18
  27.8 1.9 copy-start.9
  28.2 2.5 copy-start.17
  28.2 2.6 copy-start.7
  29.3 1.9 copy-start.10
  29.7 2.5 copy-start.16
  29.7 2.5 copy-start.4
  30.8 1.8 copy-start.11
  35.6 1.2 copy-start.1
  35.7 1.5 copy-start.3
  35.7 298.4 %all-gather.7.cloned.1.call-start = ((), (), s32[]{:S(2)}) async-start(), calls=%async_computation.3 | async-start | bytes 2162688 | tf_op jit(solution)/shard_map/all_gather | solution.py:115
  36.4 418.2 %all-reduce.2.cloned.1.call-start = ((), (), s32[]{:S(2)}) async-start(), calls=%async_computation.4 | async-start | bytes 2097152 | tf_op jit(solution)/shard_map/psum | solution.py:196
  334.1 3.7 copy-start.12
  337.2 204.8 %all-gather.9.cloned.1.call-start = ((), (), s32[]{:S(2)}) async-start(), calls=%async_computation.5 | async-start | bytes 3244032 | tf_op jit(solution)/shard_map/all_gather | solution.py:116
  340.0 205.3 %all-to-all-start = ((bf16[32,128,384]{2,1,0:T(8,128)(2,1)}), bf16[32,128,384]{2,1,0:T(8,128)(2,1)S(1)}, u32[]{:S(2)}, u32[]{:S(2)}) async-start(bf16[32,128,384]{2,1,0:T(8,128)(2,1)} %stack.23), calls=%async_computation | async-start | bytes 6291456 | tf_op jit(solution)/shard_map/all_to_all | solution.py:118
  349.8 276.9 %all-gather.11.cloned.1.call-start = ((), (), s32[]{:S(2)}) async-start(), calls=%async_computation.6 | async-start | bytes 3244032 | tf_op jit(solution)/shard_map/all_gather | solution.py:120
  350.4 191.6 %copy-start.13 = (f32[4096]{0:T(1024)S(1)}, f32[4096]{0:T(1024)}, u32[]{:S(2)}) copy-start(f32[4096]{0:T(1024)} %param.19) | copy-start | bytes 49156
  350.4 343.2 %reduce-scatter.2.cloned.1.call-start = ((), (), s32[]{:S(2)}) async-start(), calls=%async_computation.7 | async-start | bytes 1114112 | tf_op jit(solution)/shard_map/reduce_scatter | solution.py:206
Sparse Core Ops, SparseCore 0:
  35.8 184.0 all-gather.4
  222.9 77.3 all-gather.6
  337.3 117.2 all-reduce.1
  458.1 83.8 all-gather.8
  545.4 81.2 all-gather.10
  631.8 61.7 reduce-scatter.1
